TPU v7x, 32 devices: a whole 2x2x4 slice. The times are simulated.
32 devices in a mesh: gx: 4 (over y, core), gy: 2 (over x), gz: 4 (over z).
Axes of the slice: x: 2, y: 2, z: 4, core: 2. Of those that a mesh axis runs over, the one named last changes fastest.
Arguments:
- noise: float32 [32, 16, 16, 512], P(None, 'gx', 'gy', 'gz'), may hold values from -32 to 32
- basis: float32 [192, 16, 16, 512], P(None, 'gx', 'gy', 'gz'), may hold values from -5 to 5
- conductivity: float32 [16, 16, 512], P('gx', 'gy', 'gz'), may hold values from 0.2 to 2
- reaction: float32 [16, 16, 512], P('gx', 'gy', 'gz'), may hold values from 0.05 to 0.5
Outputs:
- new_block: float32 [32, 16, 16, 512], P(None, 'gx', 'gy', 'gz')
- factor: float32 [32, 32], replicated
- projection: float32 [192, 32], replicated
All inputs are finite; a program needn't handle non-finite values.
Results may differ from a plain program's by a relative error of at most 0.00012.
Values sent between devices are 32-bit elements; how exact they have to be, the bound alone decides.
A program may use at most 64 MiB of HBM per device.

v0:
```python
import jax
import jax.numpy as jnp
from jax import lax
from jax.sharding import PartitionSpec as P


def padded(value, sides, width):
    for axis, dim in sides:
        size, length = (lax.axis_size(axis), value.shape[dim])
        up = [(i, (i + 1) % size) for i in range(size - 1)]
        down = [(j, i) for i, j in up]
        last = lax.slice_in_dim(value, length - width, length, axis=dim)
        initial = lax.slice_in_dim(value, 0, width, axis=dim)
        before = lax.ppermute(last, axis, up)
        after = lax.ppermute(initial, axis, down)
        value = jnp.concatenate([before, value, after], axis=dim)
    return value


def stencil(field_pad, theta_pad, reaction_core):
    theta_core = theta_pad[1:-1, 1:-1, 1:-1]
    value_core = field_pad[:, 1:-1, 1:-1, 1:-1]
    result = reaction_core * value_core
    diagonal = reaction_core
    offsets = (
        (slice(2, None), slice(1, -1), slice(1, -1)),
        (slice(None, -2), slice(1, -1), slice(1, -1)),
        (slice(1, -1), slice(2, None), slice(1, -1)),
        (slice(1, -1), slice(None, -2), slice(1, -1)),
        (slice(1, -1), slice(1, -1), slice(2, None)),
        (slice(1, -1), slice(1, -1), slice(None, -2)),
    )
    for slicer in offsets:
        face_value = 0.5 * (theta_core + theta_pad[slicer])
        result = result + face_value * (value_core - field_pad[(slice(None),) + slicer])
        diagonal = diagonal + face_value
    return (result, diagonal)


def rim_layer(field):
    return padded(field, (("gx", 1), ("gy", 2), ("gz", 3)), 1)


def shards(noise, basis, conductivity, reaction):
    highest = lax.Precision.HIGHEST
    columns = noise.shape[0]
    span_x, span_y, span_z = (noise.shape[1], noise.shape[2], noise.shape[3])
    cell_total = float(
        span_x * span_y * span_z * lax.axis_size("gx") * lax.axis_size("gy") * lax.axis_size("gz")
    )
    extended = rim_layer(jnp.concatenate([noise, conductivity[None]], axis=0))
    theta_pad = extended[columns]
    first, diagonal = stencil(extended[:columns], theta_pad, reaction)
    image, unused = stencil(rim_layer(first / diagonal), theta_pad, reaction)
    basis_flat = basis.reshape(basis.shape[0], -1)
    image_flat = image.reshape(columns, -1)

    def local_product(left, right):
        return lax.dot_general(left, right, (((1,), (1,)), ((), ())), precision=highest)

    def remove(block, coeff):
        return block - lax.dot_general(
            coeff, basis_flat, (((0,), (0,)), ((), ())), precision=highest
        )

    def project(block):
        return lax.psum(local_product(basis_flat, block), ("gx", "gy", "gz")) / cell_total

    coeff_one = project(image_flat)
    image_one = remove(image_flat, coeff_one)
    coeff_two = project(image_one)
    image_two = remove(image_one, coeff_two)
    gram_two = lax.psum(local_product(image_two, image_two), ("gx", "gy", "gz")) / cell_total
    lower_one = jnp.linalg.cholesky(gram_two)
    middle = jax.scipy.linalg.solve_triangular(lower_one, image_two, lower=True)
    factor = lower_one.T
    return (middle.reshape(noise.shape), factor, coeff_one + coeff_two)


def solution(mesh):
    return jax.shard_map(
        shards,
        mesh=mesh,
        in_specs=(
            P(None, "gx", "gy", "gz"),
            P(None, "gx", "gy", "gz"),
            P("gx", "gy", "gz"),
            P("gx", "gy", "gz"),
        ),
        out_specs=(P(None, "gx", "gy", "gz"), P(), P()),
        check_vma=False,
    )
```

profile of v0, /device:TPU:0, one launch (start us, length us, event | category | flops | bytes accessed | tf_op | source)
XLA Modules:
  0.0 228.1 jit_solution(7743469118837655436)
XLA Ops:
  0.6 1.2 copy_dynamic-update-slice_fusion
  1.8 0.7 copy_dynamic-update-slice_fusion.1
  2.8 2.4 %collective-permute-start = (f32[33,1,8,128]{3,1,2,0:T(1,128)S(1)}, f32[33,1,8,128]{3,1,2,0:T(1,128)S(1)}, u32[]{:S(2)}, u32[]{:S(2)}) collective-permute-start(f32[33,1,8,128]{3,1,2,0:T(1,128)S(1)} %get-tuple-element.27), channel_id=1, source_target_pairs={{0,8},{8,16},{16,24},{1,9},{9,17},{17,25},{2,10},{10,18},{18,26},{... | collective-permute-start | bytes 405512 | tf_op jit(solution)/shard_map/ppermute | solution.py:14
  5.1 1.3 collective-permute-start.1
  6.4 4.1 %collective-permute-done.1 = f32[33,1,8,128]{3,1,2,0:T(1,128)S(1)} collective-permute-done((f32[33,1,8,128]{3,1,2,0:T(1,128)S(1)}, f32[33,1,8,128]{3,1,2,0:T(1,128)S(1)}, u32[]{:S(2)}, u32[]{:S(2)}) %collective-permute-start.1) | collective-permute-done | bytes 135200 | tf_op jit(solution)/shard_map/ppermute | solution.py:15
  10.6 3.4 %collective-permute-start.2 = (f32[33,6,1,128]{3,1,2,0:T(8,128)S(1)}, f32[33,6,1,128]{3,1,2,0:T(8,128)S(1)}, u32[]{:S(2)}, u32[]{:S(2)}) collective-permute-start(f32[33,6,1,128]{3,1,2,0:T(8,128)S(1)} %get-tuple-element.23), channel_id=1, source_target_pairs={{0,4},{1,5},{2,6},{3,7},{8,12},{9,13},{10,14},{11,15},{16,20},{17,... | collective-permute-start | bytes 304136 | tf_op jit(solution)/shard_map/ppermute | solution.py:14
  14.0 1.3 collective-permute-start.3
  15.3 1.2 collective-permute-done.2
  16.6 4.4 %collective-permute-done.3 = f32[33,6,1,128]{3,1,2,0:T(8,128)S(1)} collective-permute-done((f32[33,6,1,128]{3,1,2,0:T(8,128)S(1)}, f32[33,6,1,128]{3,1,2,0:T(8,128)S(1)}, u32[]{:S(2)}, u32[]{:S(2)}) %collective-permute-start.3) | collective-permute-done | bytes 101408 | tf_op jit(solution)/shard_map/ppermute | solution.py:15
  20.9 0.7 copy-done.7
  22.4 0.6 copy.37
  23.0 1.3 collective-permute-start.5
  24.9 5.1 %collective-permute-start.4 = (f32[33,6,10,1]{0,3,2,1:T(1,128)S(1)}, f32[33,6,10,1]{0,3,2,1:T(1,128)}, u32[]{:S(2)}, u32[]{:S(2)}) collective-permute-start(f32[33,6,10,1]{0,3,2,1:T(1,128)S(1)} %copy.36), channel_id=1, source_target_pairs={{0,1},{1,2},{2,3},{4,5},{5,6},{6,7},{8,9},{9,10},{10,11},{12,13},{... | collective-permute-start | bytes 23768 | tf_op jit(solution)/shard_map/ppermute | solution.py:14
  30.0 0.8 copy.39
  31.0 1.5 copy.38
  32.5 0.9 fusion.55
  33.7 5.2 %fusion.36 = f32[32,4,8,128]{3,1,2,0:T(4,128)S(1)} fusion(f32[33,6,10,1]{3,1,2,0:T(8,128)S(1)} %copy.38, f32[33,6,1,128]{3,1,2,0:T(8,128)S(1)} %copy-done.8, f32[33,6,1,128]{3,1,2,0:T(8,128)S(1)} %copy-done.6, f32[33,1,8,128]{3,1,2,0:T(1,128)S(1)} %collective-permute-done.1, f32[33,4,8,128]{3,1,2,0:T(4,128)S(1)} %copy_dynamic-update-slice_fusion.1, ...), kind=kLoop, calls=%fused_computation.55 | loop fusion | flops 4980736 | bytes 2209248 | tf_op jit(solution)/shard_map/div | solution.py:54
  39.1 3.3 %collective-permute-start.7 = (f32[32,1,8,128]{3,1,2,0:T(1,128)S(1)}, f32[32,1,8,128]{3,1,2,0:T(1,128)S(1)}, u32[]{:S(2)}, u32[]{:S(2)}) collective-permute-start(f32[32,1,8,128]{3,1,2,0:T(1,128)S(1)} %get-tuple-element.29), channel_id=1, source_target_pairs={{0,8},{8,16},{16,24},{1,9},{9,17},{17,25},{2,10},{10,18},{18,26},{... | collective-permute-start | bytes 393224 | tf_op jit(solution)/shard_map/ppermute | solution.py:14
  42.4 1.3 collective-permute-start.6
  43.7 3.5 %collective-permute-done.6 = f32[32,1,8,128]{3,1,2,0:T(1,128)S(1)} collective-permute-done((f32[32,1,8,128]{3,1,2,0:T(1,128)S(1)}, f32[32,1,8,128]{3,1,2,0:T(1,128)S(1)}, u32[]{:S(2)}, u32[]{:S(2)}) %collective-permute-start.6) | collective-permute-done | bytes 131104 | tf_op jit(solution)/shard_map/ppermute | solution.py:15
  47.3 1.5 collective-permute-start.9
  48.8 1.3 collective-permute-start.8
  50.1 1.2 collective-permute-done.9
  51.3 4.4 %collective-permute-done.8 = f32[32,6,1,128]{3,1,2,0:T(8,128)S(1)} collective-permute-done((f32[32,6,1,128]{3,1,2,0:T(8,128)S(1)}, f32[32,6,1,128]{3,1,2,0:T(8,128)S(1)}, u32[]{:S(2)}, u32[]{:S(2)}) %collective-permute-start.8) | collective-permute-done | bytes 98336 | tf_op jit(solution)/shard_map/ppermute | solution.py:15
  55.7 0.7 copy-done.9
  57.6 1.3 collective-permute-start.10
  59.5 5.1 %collective-permute-start.11 = (f32[32,6,10,1]{0,3,2,1:T(1,128)S(1)}, f32[32,6,10,1]{0,3,2,1:T(1,128)S(1)}, u32[]{:S(2)}, u32[]{:S(2)}) collective-permute-start(f32[32,6,10,1]{0,3,2,1:T(1,128)S(1)} %copy.51), channel_id=1, source_target_pairs={{0,1},{1,2},{2,3},{4,5},{5,6},{6,7},{8,9},{9,10},{10,11},{12,13},{... | collective-permute-start | bytes 23048 | tf_op jit(solution)/shard_map/ppermute | solution.py:14
  64.6 1.6 copy.50
  66.2 1.6 copy.52
  67.8 5.8 %fusion.17 = f32[32,4,8,128]{3,1,2,0:T(4,128)S(1)} fusion(f32[32,4,8,128]{3,1,2,0:T(4,128)} %copy-done.1, f32[32,6,10,1]{3,1,2,0:T(8,128)} %copy.52, f32[32,6,1,128]{3,1,2,0:T(8,128)} %copy-done.9, f32[32,6,1,128]{3,1,2,0:T(8,128)S(1)} %collective-permute-done.9, f32[32,1,8,128]{3,1,2,0:T(1,128)S(1)} %collective-permute-done.6, ...), kind=kLoop, calls=%fused_computation.18 | loop fusion | flops 4849664 | bytes 1637376 | tf_op jit(solution)/shard_map/add | solution.py:35
  73.7 0.8 copy.53
  74.5 4.3 %fusion.9 = f32[192,32]{0,1:T(8,128)S(1)} fusion(f32[192,4,8,128]{3,2,1,0:T(8,128)S(1)} %copy-done, f32[32,4,8,128]{3,1,2,0:T(4,128)S(1)} %fusion.17), kind=kOutput, calls=%fused_computation.13 | convolution fusion | flops 301989888 | bytes 3694592 | tf_op jit(solution)/shard_map/dot_general | solution.py:59
  78.8 42.2 %psum.21 = f32[192,32]{0,1:T(8,128)S(1)} all-reduce(f32[192,32]{0,1:T(8,128)S(1)} %fusion.9), channel_id=1, replica_groups=mesh['gx'=4,'gy'=2,'gz'=4] {'gx','gy','gz'}, use_global_device_ids=true, to_apply=%region_0.0 | all-reduce | flops 6144 | bytes 49152 | tf_op jit(solution)/shard_map/psum | solution.py:67
  121.0 4.8 %convolution_subtract_fusion.1 = f32[32,4096]{1,0:T(8,128)S(1)} fusion(f32[24,8,32,128]{3,2,1,0:T(8,128)S(1)} %bitcast.48, f32[4,8,32,128]{3,2,1,0:T(8,128)} %bitcast.53, f32[192,32]{0,1:T(8,128)S(1)} %psum.21), kind=kOutput, calls=%fused_computation.1 | convolution fusion | flops 302127104 | bytes 4218880 | tf_op jit(solution)/shard_map/dot_general | solution.py:62
  125.9 0.8 copy-done.3
  126.7 4.0 %fusion.12 = f32[192,32]{0,1:T(8,128)S(1)} fusion(f32[32,4096]{1,0:T(8,128)S(1)} %convolution_subtract_fusion.1, f32[24,8,32,128]{3,2,1,0:T(8,128)S(1)} %bitcast.49), kind=kOutput, calls=%fused_computation.14 | convolution fusion | flops 301989888 | bytes 3694592 | tf_op jit(solution)/shard_map/dot_general | solution.py:59
  130.7 41.9 %psum.22 = f32[192,32]{0,1:T(8,128)S(1)} all-reduce(f32[192,32]{0,1:T(8,128)S(1)} %fusion.12), channel_id=1, replica_groups=mesh['gx'=4,'gy'=2,'gz'=4] {'gx','gy','gz'}, use_global_device_ids=true, to_apply=%region_1.0 | all-reduce | flops 6144 | bytes 49152 | tf_op jit(solution)/shard_map/psum | solution.py:67
  172.6 4.7 %convolution_subtract_fusion = f32[32,4096]{1,0:T(8,128)S(1)} fusion(f32[32,4096]{1,0:T(8,128)} %copy-done.3, f32[24,8,32,128]{3,2,1,0:T(8,128)S(1)} %bitcast.50, f32[192,32]{0,1:T(8,128)S(1)} %psum.22), kind=kOutput, calls=%fused_computation | convolution fusion | flops 302127104 | bytes 4218880 | tf_op jit(solution)/shard_map/dot_general | solution.py:62
  177.4 0.7 multiply_add_fusion
  178.7 38.8 %psum.23 = f32[32,32]{0,1:T(8,128)S(1)} all-reduce(f32[32,32]{0,1:T(8,128)S(1)} %fusion.81), channel_id=1, replica_groups=mesh['gx'=4,'gy'=2,'gz'=4] {'gx','gy','gz'}, use_global_device_ids=true, to_apply=%region_2.0 | all-reduce | flops 1024 | bytes 8192 | tf_op jit(solution)/shard_map/psum | solution.py:73
  217.6 2.9 %cholesky.16 = f32[32,32]{1,0:T(8,128)S(1)} custom-call(f32[32,32]{1,0:T(8,128)S(1)} %fusion.65), custom_call_target="Cholesky" | custom-call | tf_op jit(solution)/shard_map/jit(cholesky)/cholesky | solution.py:74
  220.6 0.6 compare_reduce_fusion
  221.2 0.7 fusion.68
  221.9 0.7 copy.61
  222.5 2.4 %custom-call.7 = f32[1,32,32]{1,2,0:T(8,128)S(1)} custom-call(f32[1,32,32]{2,1,0:T(8,128)S(1)} %get-tuple-element.32), custom_call_target="InvertDiagBlocksLowerTriangular" | custom-call | tf_op jit(solution)/shard_map/jit(_solve_triangular)/triangular_solve | solution.py:75
  225.0 1.2 copy.68
  226.1 0.9 fusion.52
  227.0 1.1 copy.60
  (54 shorter events, 5.0 us)
Async XLA Ops:
  2.8 3.7 %collective-permute-start = (f32[33,1,8,128]{3,1,2,0:T(1,128)S(1)}, f32[33,1,8,128]{3,1,2,0:T(1,128)S(1)}, u32[]{:S(2)}, u32[]{:S(2)}) collective-permute-start(f32[33,1,8,128]{3,1,2,0:T(1,128)S(1)} %get-tuple-element.27), channel_id=1, source_target_pairs={{0,8},{8,16},{16,24},{1,9},{9,17},{17,25},{2,10},{10,18},{18,26},{... | collective-permute-start | bytes 405512 | tf_op jit(solution)/shard_map/ppermute | solution.py:14
  5.1 5.4 %collective-permute-start.1 = (f32[33,1,8,128]{3,1,2,0:T(1,128)S(1)}, f32[33,1,8,128]{3,1,2,0:T(1,128)S(1)}, u32[]{:S(2)}, u32[]{:S(2)}) collective-permute-start(f32[33,1,8,128]{3,1,2,0:T(1,128)S(1)} %get-tuple-element.28), channel_id=1, source_target_pairs={{8,0},{16,8},{24,16},{9,1},{17,9},{25,17},{10,2},{18,10},{26,18},{... | collective-permute-start | bytes 405512 | tf_op jit(solution)/shard_map/ppermute | solution.py:15
  10.6 5.9 %collective-permute-start.2 = (f32[33,6,1,128]{3,1,2,0:T(8,128)S(1)}, f32[33,6,1,128]{3,1,2,0:T(8,128)S(1)}, u32[]{:S(2)}, u32[]{:S(2)}) collective-permute-start(f32[33,6,1,128]{3,1,2,0:T(8,128)S(1)} %get-tuple-element.23), channel_id=1, source_target_pairs={{0,4},{1,5},{2,6},{3,7},{8,12},{9,13},{10,14},{11,15},{16,20},{17,... | collective-permute-start | bytes 304136 | tf_op jit(solution)/shard_map/ppermute | solution.py:14
  14.0 6.9 %collective-permute-start.3 = (f32[33,6,1,128]{3,1,2,0:T(8,128)S(1)}, f32[33,6,1,128]{3,1,2,0:T(8,128)S(1)}, u32[]{:S(2)}, u32[]{:S(2)}) collective-permute-start(f32[33,6,1,128]{3,1,2,0:T(8,128)S(1)} %get-tuple-element.24), channel_id=1, source_target_pairs={{4,0},{5,1},{6,2},{7,3},{12,8},{13,9},{14,10},{15,11},{20,16},{21,... | collective-permute-start | bytes 304136 | tf_op jit(solution)/shard_map/ppermute | solution.py:15
  16.6 4.4 %copy-start.5 = (f32[33,6,1,128]{3,1,2,0:T(8,128)}, f32[33,6,1,128]{3,1,2,0:T(8,128)S(1)}, u32[]{:S(2)}) copy-start(f32[33,6,1,128]{3,1,2,0:T(8,128)S(1)} %collective-permute-done.2) | copy-start | bytes 304132
  20.9 0.7 copy-start.7
  23.0 7.0 %collective-permute-start.5 = (f32[33,6,10,1]{0,3,2,1:T(1,128)S(1)}, f32[33,6,10,1]{0,3,2,1:T(1,128)S(1)}, u32[]{:S(2)}, u32[]{:S(2)}) collective-permute-start(f32[33,6,10,1]{0,3,2,1:T(1,128)S(1)} %copy.37), channel_id=1, source_target_pairs={{1,0},{2,1},{3,2},{5,4},{6,5},{7,6},{9,8},{10,9},{11,10},{13,12},{... | collective-permute-start | bytes 23768 | tf_op jit(solution)/shard_map/ppermute | solution.py:15
  24.9 6.1 %collective-permute-start.4 = (f32[33,6,10,1]{0,3,2,1:T(1,128)S(1)}, f32[33,6,10,1]{0,3,2,1:T(1,128)}, u32[]{:S(2)}, u32[]{:S(2)}) collective-permute-start(f32[33,6,10,1]{0,3,2,1:T(1,128)S(1)} %copy.36), channel_id=1, source_target_pairs={{0,1},{1,2},{2,3},{4,5},{5,6},{6,7},{8,9},{9,10},{10,11},{12,13},{... | collective-permute-start | bytes 23768 | tf_op jit(solution)/shard_map/ppermute | solution.py:14
  32.5 1.0 copy-start.16
  32.5 1.1 copy-start.4
  32.5 1.1 copy-start.6
  32.5 1.1 copy-start.8
  33.6 5.3 %copy-start.10 = (f32[4,8,128]{2,0,1:T(4,128)}, f32[4,8,128]{2,0,1:T(4,128)S(1)}, u32[]{:S(2)}) copy-start(f32[4,8,128]{2,0,1:T(4,128)S(1)} %get-tuple-element.14) | copy-start | bytes 49156
  33.6 5.3 %copy-start.11 = (f32[4,8,128]{2,0,1:T(4,128)}, f32[4,8,128]{2,0,1:T(4,128)S(1)}, u32[]{:S(2)}) copy-start(f32[4,8,128]{2,0,1:T(4,128)S(1)} %get-tuple-element.15) | copy-start | bytes 49156
  33.6 5.3 %copy-start.12 = (f32[4,8,128]{2,0,1:T(4,128)}, f32[4,8,128]{2,0,1:T(4,128)S(1)}, u32[]{:S(2)}) copy-start(f32[4,8,128]{2,0,1:T(4,128)S(1)} %get-tuple-element.16) | copy-start | bytes 49156
  33.6 5.3 %copy-start.13 = (f32[4,8,128]{2,0,1:T(4,128)}, f32[4,8,128]{2,0,1:T(4,128)S(1)}, u32[]{:S(2)}) copy-start(f32[4,8,128]{2,0,1:T(4,128)S(1)} %get-tuple-element.17) | copy-start | bytes 49156
  33.6 5.3 %copy-start.14 = (f32[4,8,128]{2,0,1:T(4,128)}, f32[4,8,128]{2,0,1:T(4,128)S(1)}, u32[]{:S(2)}) copy-start(f32[4,8,128]{2,0,1:T(4,128)S(1)} %get-tuple-element.18) | copy-start | bytes 49156
  33.6 5.3 %copy-start.15 = (f32[4,8,128]{2,0,1:T(4,128)}, f32[4,8,128]{2,0,1:T(4,128)S(1)}, u32[]{:S(2)}) copy-start(f32[4,8,128]{2,0,1:T(4,128)S(1)} %get-tuple-element.33) | copy-start | bytes 49156
  38.9 16.8 %copy-start.1 = (f32[32,4,8,128]{3,1,2,0:T(4,128)}, f32[32,4,8,128]{3,1,2,0:T(4,128)S(1)}, u32[]{:S(2)}) copy-start(f32[32,4,8,128]{3,1,2,0:T(4,128)S(1)} %fusion.36) | copy-start | bytes 1572868
  39.1 4.6 %collective-permute-start.7 = (f32[32,1,8,128]{3,1,2,0:T(1,128)S(1)}, f32[32,1,8,128]{3,1,2,0:T(1,128)S(1)}, u32[]{:S(2)}, u32[]{:S(2)}) collective-permute-start(f32[32,1,8,128]{3,1,2,0:T(1,128)S(1)} %get-tuple-element.29), channel_id=1, source_target_pairs={{0,8},{8,16},{16,24},{1,9},{9,17},{17,25},{2,10},{10,18},{18,26},{... | collective-permute-start | bytes 393224 | tf_op jit(solution)/shard_map/ppermute | solution.py:14
  42.4 4.8 %collective-permute-start.6 = (f32[32,1,8,128]{3,1,2,0:T(1,128)S(1)}, f32[32,1,8,128]{3,1,2,0:T(1,128)S(1)}, u32[]{:S(2)}, u32[]{:S(2)}) collective-permute-start(f32[32,1,8,128]{3,1,2,0:T(1,128)S(1)} %get-tuple-element.30), channel_id=1, source_target_pairs={{8,0},{16,8},{24,16},{9,1},{17,9},{25,17},{10,2},{18,10},{26,18},{... | collective-permute-start | bytes 393224 | tf_op jit(solution)/shard_map/ppermute | solution.py:15
  47.3 4.0 %collective-permute-start.9 = (f32[32,6,1,128]{3,1,2,0:T(8,128)S(1)}, f32[32,6,1,128]{3,1,2,0:T(8,128)S(1)}, u32[]{:S(2)}, u32[]{:S(2)}) collective-permute-start(f32[32,6,1,128]{3,1,2,0:T(8,128)S(1)} %get-tuple-element.25), channel_id=1, source_target_pairs={{0,4},{1,5},{2,6},{3,7},{8,12},{9,13},{10,14},{11,15},{16,20},{17,... | collective-permute-start | bytes 294920 | tf_op jit(solution)/shard_map/ppermute | solution.py:14
  48.8 6.9 %collective-permute-start.8 = (f32[32,6,1,128]{3,1,2,0:T(8,128)S(1)}, f32[32,6,1,128]{3,1,2,0:T(8,128)S(1)}, u32[]{:S(2)}, u32[]{:S(2)}) collective-permute-start(f32[32,6,1,128]{3,1,2,0:T(8,128)S(1)} %get-tuple-element.26), channel_id=1, source_target_pairs={{4,0},{5,1},{6,2},{7,3},{12,8},{13,9},{14,10},{15,11},{20,16},{21,... | collective-permute-start | bytes 294920 | tf_op jit(solution)/shard_map/ppermute | solution.py:15
  55.7 0.7 copy-start.9
  57.6 6.9 %collective-permute-start.10 = (f32[32,6,10,1]{0,3,2,1:T(1,128)S(1)}, f32[32,6,10,1]{0,3,2,1:T(1,128)S(1)}, u32[]{:S(2)}, u32[]{:S(2)}) collective-permute-start(f32[32,6,10,1]{0,3,2,1:T(1,128)S(1)} %copy.49), channel_id=1, source_target_pairs={{1,0},{2,1},{3,2},{5,4},{6,5},{7,6},{9,8},{10,9},{11,10},{13,12},{... | collective-permute-start | bytes 23048 | tf_op jit(solution)/shard_map/ppermute | solution.py:15
  59.5 6.8 %collective-permute-start.11 = (f32[32,6,10,1]{0,3,2,1:T(1,128)S(1)}, f32[32,6,10,1]{0,3,2,1:T(1,128)S(1)}, u32[]{:S(2)}, u32[]{:S(2)}) collective-permute-start(f32[32,6,10,1]{0,3,2,1:T(1,128)S(1)} %copy.51), channel_id=1, source_target_pairs={{0,1},{1,2},{2,3},{4,5},{5,6},{6,7},{8,9},{9,10},{10,11},{12,13},{... | collective-permute-start | bytes 23048 | tf_op jit(solution)/shard_map/ppermute | solution.py:14
  67.8 6.7 %copy-start = (f32[192,4,8,128]{3,2,1,0:T(8,128)S(1)}, f32[192,4,8,128]{3,2,1,0:T(8,128)}, u32[]{:S(2)}) copy-start(f32[192,4,8,128]{3,2,1,0:T(8,128)} %param.5) | copy-start | bytes 9437188
  125.9 0.8 copy-start.3
  177.3 0.8 copy-start.2
where the time goes:
time: 229 us; the launch traced here: 228 us
  blocking collectives  123 us (54%)
  starting transfers between devices  28.6 us (12%)
  other arithmetic  20.3 us (9%)
  matrix products  19.3 us (8%)
  waiting for transfers between devices  18.9 us (8%)
  local copies, waits for them, and re-layouts  17 us (7%)
    psum x2, blocking collectives, project(): lax.psum(local_product(basis_flat, block), ('gx', 'gy', 'gz')) / cell_total  84.1 us
    psum x1, blocking collectives, shards(): lax.psum(local_product(image_two, image_two), ('gx', 'gy', 'gz'))  38.8 us
    ppermute x6, starting transfers between devices, padded(): before = lax.ppermute(last, axis, up)  20.8 us
    ppermute x6, waiting for transfers between devices, padded(): after = lax.ppermute(initial, axis, down)  16.3 us
    dot_general x2, matrix products, remove(): lax.dot_general(coeff, basis_flat, (((0,), (0,)), ((), ())), precision=hi...  9.56 us
    dot_general x3, matrix products, local_product(): lax.dot_general(left, right, (((1,), (1,)), ((), ())), precision=highest)  8.9 us
    ppermute x6, starting transfers between devices, padded(): after = lax.ppermute(initial, axis, down)  7.74 us
    unnamed x38, local copies, waits for them, and re-layouts  6.42 us
  transfers between devices with their start and end apart: 12, of which 7 were waited for; matrix products, arithmetic and copies ran while one was open for 2% of the time, Pallas kernels for 0%

commit v1 on v0

v1 whole, which is shorter than its diff:
```python
import functools

import jax
import jax.numpy as jnp
from jax import lax
from jax.experimental import pallas as pl
from jax.experimental.pallas import tpu as pltpu
from jax.sharding import PartitionSpec as P

MESH = pl.DeviceIdType.MESH
GROUP = 8
F32 = jnp.float32
BF16 = jnp.bfloat16


def each(count, body):
    if count <= 8:
        for k in range(1, count):
            body(k)
    else:
        lax.fori_loop(1, count, lambda k, c: (body(k), c)[1], 0)


class Team:
    def __init__(self, axes, sizes):
        self.axes = axes
        self.sizes = sizes
        self.count = 1
        for axis in axes:
            self.count *= sizes[axis]

    def me(self):
        index = 0
        for axis in self.axes:
            index = index * self.sizes[axis] + lax.axis_index(axis)
        return index

    def device(self, index):
        out = {}
        for axis in reversed(self.axes):
            out[axis] = lax.rem(index, self.sizes[axis])
            index = lax.div(index, self.sizes[axis])
        return out

    def peer(self, k):
        return lax.rem(self.me() + k, self.count)


class Sum:
    def __init__(self, owners, others, data, landed, crossed, result, sems):
        self.owners, self.others = owners, others
        self.data, self.landed, self.crossed, self.result = data, landed, crossed, result
        self.sems = sems
        self.share = data.shape[0] // owners.count

    def copy(self, phase, team, src, dst_ref, slot, peer):
        send, recv = self.sems[2 * phase], self.sems[2 * phase + 1]
        return pltpu.make_async_remote_copy(
            src_ref=src,
            dst_ref=dst_ref.at[slot],
            send_sem=send.at[peer],
            recv_sem=recv.at[slot],
            device_id=team.device(peer),
            device_id_type=MESH,
        )

    def piece(self, index):
        return self.data.at[pl.ds(index * self.share, self.share)]

    def scatter(self):
        team, me = self.owners, self.owners.me()

        def go(k):
            peer = team.peer(k)
            self.copy(0, team, self.piece(peer), self.landed, me, peer).start()

        each(team.count, go)
        self.landed[me] = self.data[pl.ds(me * self.share, self.share)]

    def settle(self, phase, team, src, dst_ref):
        def go(k):
            peer = team.peer(k)
            self.copy(phase, team, src, dst_ref, peer, peer).wait_recv()

        each(team.count, go)

    def cross(self):
        self.settle(0, self.owners, self.piece(0), self.landed)
        team, me = self.others, self.others.me()
        total = self.landed[0]
        for k in range(1, self.owners.count):
            total = total + self.landed[k]
        self.crossed[me] = total

        def go(k):
            peer = team.peer(k)
            self.copy(1, team, self.crossed.at[me], self.crossed, me, peer).start()

        each(team.count, go)

    def gather(self):
        self.settle(1, self.others, self.crossed.at[0], self.crossed)
        team, me = self.owners, self.owners.me()
        total = self.crossed[0]
        for k in range(1, self.others.count):
            total = total + self.crossed[k]
        self.result[me] = total

        def go(k):
            peer = team.peer(k)
            self.copy(2, team, self.result.at[me], self.result, me, peer).start()

        each(team.count, go)

    def finish(self):
        self.settle(2, self.owners, self.result.at[0], self.result)

    def drain(self):
        def scattered(k):
            peer = self.owners.peer(k)
            self.copy(0, self.owners, self.piece(0), self.landed, 0, peer).wait_send()

        def crossed(k):
            peer = self.others.peer(k)
            self.copy(1, self.others, self.crossed.at[0], self.crossed, 0, peer).wait_send()

        def gathered(k):
            peer = self.owners.peer(k)
            self.copy(2, self.owners, self.result.at[0], self.result, 0, peer).wait_send()

        each(self.owners.count, scattered)
        each(self.others.count, crossed)
        each(self.owners.count, gathered)


class Rim:
    def __init__(self, field, x_in, y_out, y_in, z_out, z_in, send, recv, sizes):
        self.sizes = sizes
        self.send, self.recv = send, recv
        last = field.shape[1] - 1
        self.routes = (
            ("gx", (field.at[:, 0], field.at[:, last]), x_in),
            ("gy", (y_out.at[0], y_out.at[1]), y_in),
            ("gz", (z_out.at[0], z_out.at[1]), z_in),
        )

    def exists(self, axis, side):
        me = lax.axis_index(axis)
        return me > 0 if side == 0 else me < self.sizes[axis] - 1

    def copy(self, at, side):
        axis, out, into = self.routes[at]
        me = lax.axis_index(axis)
        step = -1 if side == 0 else 1
        return pltpu.make_async_remote_copy(
            src_ref=out[side],
            dst_ref=into.at[1 - side],
            send_sem=self.send.at[2 * at + side],
            recv_sem=self.recv.at[2 * at + 1 - side],
            device_id={axis: me + step},
            device_id_type=MESH,
        )

    def start(self, at):
        axis = self.routes[at][0]
        for side in range(2):
            pl.when(self.exists(axis, side))(lambda at=at, side=side: self.copy(at, side).start())

    def blank(self):
        for axis, _, into in self.routes:
            for side in range(2):
                @pl.when(jnp.logical_not(self.exists(axis, side)))
                def _(into=into, side=side):
                    into[side] = jnp.zeros(into.shape[1:], F32)

    def arrive(self):
        for at in range(3):
            axis = self.routes[at][0]
            for side in range(2):
                pl.when(self.exists(axis, side))(
                    lambda at=at, side=side: self.copy(at, 1 - side).wait_recv()
                )

    def drain(self):
        for at in range(3):
            axis = self.routes[at][0]
            for side in range(2):
                pl.when(self.exists(axis, side))(
                    lambda at=at, side=side: self.copy(at, side).wait_send()
                )


def lanes_of(shape):
    return lax.broadcasted_iota(jnp.int32, shape, len(shape) - 1)


def pack_y(flat, rows, y_out):
    for side, first in ((0, 0), (1, 7)):
        y_out[side, pl.ds(0, rows), :] = flat[pl.ds(first, rows, stride=8), :]


def pack_z(tiles, lanes_total):
    lane = lanes_of((8, 128))
    lo = jnp.zeros((8, 128), F32)
    hi = jnp.zeros((8, 128), F32)
    for i in range(lanes_total):
        tile = tiles[i]
        lo = jnp.where(lane == i, jnp.broadcast_to(tile[:, 0:1], (8, 128)), lo)
        hi = jnp.where(lane == i, jnp.broadcast_to(tile[:, 127:128], (8, 128)), hi)
    return lo, hi


def neighbours(value, x_lo, x_hi, y_lo, y_hi, z_lo, z_hi):
    count, span = value.shape[0], value.shape[1]
    tiles = count * span
    flat = value.reshape(tiles, 8, 128)
    below = jnp.concatenate([x_lo[:, None], value[:, : span - 1]], axis=1)
    above = jnp.concatenate([value[:, 1:], x_hi[:, None]], axis=1)
    row = lax.broadcasted_iota(jnp.int32, (8, 128), 0)
    lane = lanes_of((8, 128))
    before, after, left, right = [], [], [], []
    for i in range(tiles):
        tile = flat[i]
        before.append(
            jnp.where(row == 0, jnp.broadcast_to(y_lo[i], (8, 128)), pltpu.roll(tile, 1, 0))
        )
        after.append(
            jnp.where(row == 7, jnp.broadcast_to(y_hi[i], (8, 128)), pltpu.roll(tile, 7, 0))
        )
        left.append(
            jnp.where(lane == 0, jnp.broadcast_to(z_lo[:, i : i + 1], (8, 128)), pltpu.roll(tile, 1, 1))
        )
        right.append(
            jnp.where(
                lane == 127, jnp.broadcast_to(z_hi[:, i : i + 1], (8, 128)), pltpu.roll(tile, 127, 1)
            )
        )
    join = lambda parts: jnp.stack(parts).reshape(value.shape)
    return above, below, join(after), join(before), join(right), join(left)


def split(value):
    high = value.astype(BF16)
    return high, (value - high.astype(F32)).astype(BF16)


def dot(left, right, dims):
    return lax.dot_general(left, right, (dims, ((), ())), preferred_element_type=F32)


def dot_full(left, right, dims):
    return lax.dot_general(
        left, right, (dims, ((), ())), precision=lax.Precision.HIGHEST, preferred_element_type=F32
    )


NT = ((1,), (1,))
NN = ((1,), (0,))


def kernel(sizes, owners, others, cell_total, noise, basis, cond, react, out, factor, proj, *scratch):
    (field, field2, image, stored, react_v, coef, high, low, flat_image, residual, chol,
     x_in1, x_in2, y_out1, y_in1, y_out2, y_in2, z_out1, z_in1, z_out2, z_in2,
     c_data, c_landed, c_crossed, c_result, g_data, g_landed, g_crossed, g_result,
     in_sems, h_send1, h_recv1, h_send2, h_recv2, *sum_sems) = scratch
    columns, span = field2.shape[0], field2.shape[1]
    plane = span * 8
    kept = basis.shape[0] // plane
    cells = plane * 128
    tiles = columns * span
    scale = 1.0 / cell_total

    load_noise = pltpu.make_async_copy(noise, field.at[pl.ds(0, columns)], in_sems.at[0])
    load_cond = pltpu.make_async_copy(cond, field.at[columns], in_sems.at[1])
    load_react = pltpu.make_async_copy(react, react_v, in_sems.at[2])
    load_basis = pltpu.make_async_copy(basis, stored, in_sems.at[3])
    load_noise.start()
    load_cond.start()
    load_react.start()
    load_basis.start()

    barrier = pltpu.get_barrier_semaphore()
    for team in (owners, others):
        def greet(k, team=team):
            pl.semaphore_signal(
                barrier, inc=1, device_id=team.device(team.peer(k)), device_id_type=MESH
            )
        each(team.count, greet)

    rim1 = Rim(field, x_in1, y_out1, y_in1, z_out1, z_in1, h_send1, h_recv1, sizes)
    rim2 = Rim(field2, x_in2, y_out2, y_in2, z_out2, z_in2, h_send2, h_recv2, sizes)
    rim1.blank()
    rim2.blank()
    load_noise.wait()
    load_cond.wait()
    pl.semaphore_wait(barrier, owners.count + others.count - 2)
    rim1.start(0)
    field_flat = field.reshape((columns + 1) * plane, 128)
    y_rows = tiles + span
    y_out1[...] = jnp.zeros(y_out1.shape, F32)
    pack_y(field_flat, y_rows, y_out1)
    rim1.start(1)
    lo, hi = pack_z(field[0:columns].reshape(tiles, 8, 128), tiles)
    z_out1[0, 0], z_out1[1, 0] = lo, hi
    lo, hi = pack_z(field[columns], span)
    z_out1[0, 1], z_out1[1, 1] = lo, hi
    rim1.start(2)

    load_basis.wait()
    spare = high.shape[0] - kept
    high[kept:, :] = jnp.zeros((spare, cells), BF16)
    low[kept:, :] = jnp.zeros((spare, cells), BF16)
    for at in range(plane):
        one, two = split(stored[pl.ds(at, kept, stride=plane), :])
        high[0:kept, at * 128 : (at + 1) * 128] = one
        low[0:kept, at * 128 : (at + 1) * 128] = two

    chunk = 1024
    g_one = jnp.zeros((kept, 256), F32)
    g_two = jnp.zeros((kept, 256), F32)
    for at in range(0, cells, chunk):
        right = high[:, at : at + chunk]
        g_one = g_one + dot(high[0:kept, at : at + chunk], right, NT)
        g_two = g_two + dot(low[0:kept, at : at + chunk], right, NT)
    turned = jnp.transpose(jnp.concatenate([g_two, jnp.zeros((256 - kept, 256), F32)], axis=0))
    g_local = g_one + g_two + turned[0:kept]
    for at in range(kept // 8):
        for half in range(2):
            g_data[2 * at + half] = g_local[8 * at : 8 * at + 8, 128 * half : 128 * half + 128]

    c_sum = Sum(owners, others, c_data, c_landed, c_crossed, c_result, sum_sems[0:6])
    g_sum = Sum(owners, others, g_data, g_landed, g_crossed, g_result, sum_sems[6:12])
    g_sum.scatter()

    load_react.wait()
    rim1.arrive()
    theta = field[columns]
    around = neighbours(
        theta[None],
        x_in1[0, columns][None],
        x_in1[1, columns][None],
        [y_in1[0, pl.ds(tiles + i, 1), :] for i in range(span)],
        [y_in1[1, pl.ds(tiles + i, 1), :] for i in range(span)],
        z_in1[0, 1],
        z_in1[1, 1],
    )
    diagonal = react_v[...]
    for face, other in enumerate(around):
        value = 0.5 * (theta + other[0])
        coef[face] = value
        diagonal = diagonal + value
    coef[6] = diagonal

    def apply(source, x_in, y_in, z_in, group):
        start = group * GROUP
        value = source[pl.ds(start, GROUP)]
        shift = lax.rem(128 - group * (GROUP * span), 128)
        first = start * span
        around = neighbours(
            value,
            x_in[0, pl.ds(start, GROUP)],
            x_in[1, pl.ds(start, GROUP)],
            [y_in[0, pl.ds(first + i, 1), :] for i in range(GROUP * span)],
            [y_in[1, pl.ds(first + i, 1), :] for i in range(GROUP * span)],
            pltpu.roll(z_in[0, 0], shift, 1),
            pltpu.roll(z_in[1, 0], shift, 1),
        )
        result = react_v[...][None] * value
        for face, other in enumerate(around):
            result = result + coef[face][None] * (value - other)
        return start, result

    def first_step(group, carry):
        start, result = apply(field, x_in1, y_in1, z_in1, group)
        field2[pl.ds(start, GROUP)] = result / coef[6][None]
        return carry

    lax.fori_loop(0, columns // GROUP, first_step, 0)
    rim2.start(0)
    pack_y(field2.reshape(columns * plane, 128), tiles, y_out2)
    rim2.start(1)
    lo, hi = pack_z(field2[...].reshape(tiles, 8, 128), tiles)
    z_out2[0, 0], z_out2[1, 0] = lo, hi
    rim2.start(2)
    g_sum.cross()
    rim2.arrive()

    def second_step(group, carry):
        start, result = apply(field2, x_in2, y_in2, z_in2, group)
        image[pl.ds(start, GROUP)] = result
        return carry

    lax.fori_loop(0, columns // GROUP, second_step, 0)
    image_rows = image.reshape(columns * plane, 128)
    for at in range(plane):
        value = image_rows[pl.ds(at, columns, stride=plane), :]
        flat_image[:, at * 128 : (at + 1) * 128] = value
        one, two = split(value)
        high[kept : kept + columns, at * 128 : (at + 1) * 128] = one
        low[kept : kept + columns, at * 128 : (at + 1) * 128] = two

    both = jnp.zeros((2 * columns, 256), F32)
    for at in range(0, cells, chunk):
        here = slice(at, at + chunk)
        left = jnp.concatenate([high[kept : kept + columns, here], low[kept : kept + columns, here]], axis=0)
        both = both + dot(left, high[:, here], NT) + dot(left, low[:, here], NT)
    c_local = both[0:columns] + both[columns:]
    for at in range(columns // 8):
        for half in range(2):
            c_data[2 * at + half] = c_local[8 * at : 8 * at + 8, 128 * half : 128 * half + 128]
    c_sum.scatter()
    g_sum.gather()
    c_sum.cross()
    c_sum.gather()
    g_sum.finish()
    c_sum.finish()

    def whole(total, rows):
        tiles_of = total[...].reshape(rows // 4, 8, 128)
        return jnp.concatenate(
            [
                jnp.concatenate([tiles_of[2 * at], tiles_of[2 * at + 1]], axis=1)
                for at in range(rows // 8)
            ],
            axis=0,
        )

    g_full = jnp.concatenate(
        [whole(g_result, kept) * scale, jnp.zeros((256 - kept, 256), F32)], axis=0
    )
    c_full = whole(c_result, columns) * scale
    lane = lanes_of((columns, 256))
    c_one = jnp.where(lane < kept, c_full, 0.0)
    square = c_full[:, kept : kept + columns]
    total = 2.0 * c_one - dot_full(c_one, g_full, NN)
    rest = c_one - dot_full(total, g_full, NN)
    gram = square - dot_full(c_one, total, NT) - dot_full(total, rest, NT)
    proj[...] = jnp.transpose(total)[0:kept, :]

    p_high, p_low = split(total)
    p_both = jnp.concatenate([p_high, p_low], axis=0)[:, 0:kept]
    for at in range(0, cells, chunk):
        here = slice(at, at + chunk)
        part = dot(p_both, high[0:kept, here], NN) + dot(p_both, low[0:kept, here], NN)
        residual[:, here] = flat_image[:, here] - part[0:columns] - part[columns:]

    wide = (columns, 128)
    lane = lanes_of(wide)
    row = lax.broadcasted_iota(jnp.int32, wide, 0)
    table = jnp.where(lane == row + columns, 1.0, 0.0).astype(F32)
    table = table + jnp.concatenate([gram, jnp.zeros((columns, 128 - columns), F32)], axis=1)
    for k in range(columns):
        column = jnp.broadcast_to(table[:, k : k + 1], wide)
        root = lax.rsqrt(column[k : k + 1, :])
        line = table[k : k + 1, :] * root
        chol[k : k + 1, :] = line
        table = table - (column * root) * line
    done = chol[...]
    factor[...] = jnp.where(lane >= row, done, 0.0)[:, 0:columns]
    inverse = done[:, columns : 2 * columns]
    for at in range(0, cells, chunk):
        here = slice(at, at + chunk)
        part = dot_full(inverse, residual[:, here], NN)
        for k in range(chunk // 128):
            out[pl.ds(at // 128 + k, columns, stride=plane), :] = part[:, 128 * k : 128 * k + 128]

    rim1.drain()
    rim2.drain()
    g_sum.drain()
    c_sum.drain()


def shards(sizes, noise, basis, cond, react):
    columns, span, rows, lanes = noise.shape
    kept = basis.shape[0]
    plane = span * rows
    cells = plane * lanes
    cell_total = float(cells * sizes["gx"] * sizes["gy"] * sizes["gz"])
    c_tiles, g_tiles = columns // 4, kept // 4
    own, rest, count = [], [], 1
    for axis in ("gx", "gy", "gz"):
        if c_tiles % (count * sizes[axis]) == 0:
            count *= sizes[axis]
            own.append(axis)
        else:
            rest.append(axis)
    owners, others = Team(own, sizes), Team(rest, sizes)
    vmem = lambda *shape: pltpu.VMEM(shape, F32)
    y_rows = -(-(columns + 1) * span // 8) * 8

    def sum_buffers(tiles):
        share = tiles // owners.count
        return [
            vmem(tiles, 8, 128),
            vmem(owners.count, share, 8, 128),
            vmem(others.count, share, 8, 128),
            vmem(owners.count, share, 8, 128),
        ]

    dma = lambda n: pltpu.SemaphoreType.DMA((n,))
    sum_sems = [dma(n) for n in (owners.count, owners.count, others.count, others.count, owners.count, owners.count)]
    scratch = [
        vmem(columns + 1, span, 8, 128),
        vmem(columns, span, 8, 128),
        vmem(columns, span, 8, 128),
        vmem(kept * plane, 128),
        vmem(span, 8, 128),
        vmem(7, span, 8, 128),
        pltpu.VMEM((256, cells), BF16),
        pltpu.VMEM((256, cells), BF16),
        vmem(columns, cells),
        vmem(columns, cells),
        vmem(columns, 128),
        vmem(2, columns + 1, 8, 128),
        vmem(2, columns, 8, 128),
        vmem(2, y_rows, 128),
        vmem(2, y_rows, 128),
        vmem(2, columns * span, 128),
        vmem(2, columns * span, 128),
        vmem(2, 2, 8, 128),
        vmem(2, 2, 8, 128),
        vmem(2, 1, 8, 128),
        vmem(2, 1, 8, 128),
        *sum_buffers(c_tiles),
        *sum_buffers(g_tiles),
        dma(4),
        dma(6),
        dma(6),
        dma(6),
        dma(6),
        *sum_sems,
        *sum_sems,
    ]
    out, factor, proj = pl.pallas_call(
        functools.partial(kernel, sizes, owners, others, cell_total),
        out_shape=(
            jax.ShapeDtypeStruct((columns * plane, lanes), F32),
            jax.ShapeDtypeStruct((columns, columns), F32),
            jax.ShapeDtypeStruct((kept, columns), F32),
        ),
        in_specs=[pl.BlockSpec(memory_space=pl.ANY)] * 4,
        out_specs=tuple([pl.BlockSpec(memory_space=pltpu.VMEM)] * 3),
        scratch_shapes=scratch,
        compiler_params=pltpu.CompilerParams(
            collective_id=0, has_side_effects=True, vmem_limit_bytes=48 * 1024 * 1024
        ),
        name="lanczos_step",
    )(noise, basis.reshape(kept * plane, lanes), cond, react)
    return out.reshape(noise.shape), factor, proj


def solution(mesh):
    sizes = dict(mesh.shape)
    return jax.shard_map(
        functools.partial(shards, sizes),
        mesh=mesh,
        in_specs=(
            P(None, "gx", "gy", "gz"),
            P(None, "gx", "gy", "gz"),
            P("gx", "gy", "gz"),
            P("gx", "gy", "gz"),
        ),
        out_specs=(P(None, "gx", "gy", "gz"), P(), P()),
        check_vma=False,
    )
```

time: 229 us -> 40.5 us (0.18)
  blocking collectives: 123 us -> 0 us
  Pallas kernels: 0 us -> 33.1 us
  starting transfers between devices: 28.6 us -> 0 us
  other arithmetic: 20.3 us -> 0 us
  matrix products: 19.3 us -> 0 us
  waiting for transfers between devices: 18.9 us -> 0 us
  local copies, waits for them, and re-layouts: 17 us -> 6.45 us
    psum x3 -> x0, blocking collectives: 123 us -> none  [the longest x2 84.1 us: project(): lax.psum(local_product(basis_flat, block), ('gx', 'gy', 'gz')) / cell_total]
    pallas_call x0 -> x1, Pallas kernels: none -> 33.1 us  [shards(): pl.pallas_call(functools.partial(kernel, sizes, owners, others, cell_tota...]
    ppermute x12 -> x0, starting transfers between devices: 28.6 us -> none  [the longest x6 20.8 us: padded(): before = lax.ppermute(last, axis, up)]
    ppermute x12 -> x0, waiting for transfers between devices: 18.9 us -> none  [the longest x6 16.3 us: padded(): after = lax.ppermute(initial, axis, down)]
    dot_general x5 -> x0, matrix products: 18.5 us -> none  [the longest x2 9.56 us: remove(): lax.dot_general(coeff, basis_flat, (((0,), (0,)), ((), ())), precision=hi...]
    add x3 -> x0, other arithmetic: 6.63 us -> none  [the longest x1 5.84 us: stencil(): result + face_value * (value_core - field_pad[(slice(None),) + slicer])]
    another operation x4 -> x0, other arithmetic: 6.03 us -> none  [the longest x3 3.6 us: shards(): lower_one = jnp.linalg.cholesky(gram_two)]
    ppermute x4 -> x0, local copies, waits for them, and re-layouts: 5.5 us -> none  [the longest x2 3.13 us: padded(): before = lax.ppermute(last, axis, up)]
  transfers between devices with their start and end apart: 12 -> 0, of which waited for: 7 -> 0; matrix products, arithmetic and copies ran while one was open for 2% -> 0% of each run, Pallas kernels for 0% -> 0%
where the time goes in v1:
time: 40.5 us; the launch traced here: 40.2 us
  Pallas kernels  33.1 us (82%)
  local copies, waits for them, and re-layouts  6.45 us (16%)
  between operations  0.65 us (2%)
    pallas_call x1, Pallas kernels, shards(): pl.pallas_call(functools.partial(kernel, sizes, owners, others, cell_tota...  33.1 us
    unnamed x11, local copies, waits for them, and re-layouts  6.45 us

profile of v1, /device:TPU:0, one launch (start us, length us, event | category | flops | bytes accessed | tf_op | source)
XLA Modules:
  0.0 40.2 jit_solution(15196478883177712566)
XLA Ops:
  0.6 0.0 copy-start
  0.6 1.9 %copy-done = f32[192,4,8,128]{3,2,1,0:T(8,128)S(1)} copy-done((f32[192,4,8,128]{3,2,1,0:T(8,128)S(1)}, f32[192,4,8,128]{3,2,1,0:T(8,128)}, u32[]{:S(2)}) %copy-start) | copy-done | bytes 3145752
  2.5 0.0 copy-start.1
  2.5 1.0 %copy-done.1 = f32[32,4,8,128]{3,2,1,0:T(8,128)S(1)} copy-done((f32[32,4,8,128]{3,2,1,0:T(8,128)S(1)}, f32[32,4,8,128]{3,2,1,0:T(8,128)}, u32[]{:S(2)}) %copy-start.1) | copy-done | bytes 524312
  3.6 0.0 copy-start.2
  3.6 0.7 %copy-done.2 = f32[4,8,128]{2,1,0:T(8,128)S(1)} copy-done((f32[4,8,128]{2,1,0:T(8,128)S(1)}, f32[4,8,128]{2,1,0:T(8,128)}, u32[]{:S(2)}) %copy-start.2) | copy-done | bytes 16408
  4.3 0.0 copy-start.3
  4.3 0.7 %copy-done.3 = f32[4,8,128]{2,1,0:T(8,128)S(1)} copy-done((f32[4,8,128]{2,1,0:T(8,128)S(1)}, f32[4,8,128]{2,1,0:T(8,128)}, u32[]{:S(2)}) %copy-start.3) | copy-done | bytes 16408
  5.0 33.1 %lanczos_step.1 = (f32[1024,128]{1,0:T(8,128)S(1)}, f32[32,32]{1,0:T(8,128)S(1)}, f32[192,32]{1,0:T(8,128)S(1)}) custom-call(f32[32,4,8,128]{3,2,1,0:T(8,128)S(1)} %copy-done.1, f32[6144,128]{1,0:T(8,128)S(1)} %bitcast.2, f32[4,8,128]{2,1,0:T(8,128)S(1)} %copy-done.2, f32[4,8,128]{2,1,0:T(8,128)S(1)} %copy-done.3), custom_call_target="tpu_custom_call" | custom-call | tf_op jit(solution)/shard_map/lanczos_step/pallas_call | solution.py:534
  38.1 0.7 %copy.7 = f32[192,32]{0,1:T(8,128)} copy(f32[192,32]{1,0:T(8,128)S(1)} %get-tuple-element.11) | data formatting | bytes 49152
  38.8 0.8 %copy.10 = f32[32,4,8,128]{3,2,1,0:T(8,128)} copy(f32[32,4,8,128]{3,2,1,0:T(8,128)S(1)} %bitcast.3) | data formatting | bytes 1048576
  39.6 0.6 %copy.11 = f32[32,32]{1,0:T(8,128)} copy(f32[32,32]{1,0:T(8,128)S(1)} %get-tuple-element.16) | data formatting | bytes 8192
Async XLA Ops:
  0.6 1.9 %copy-start = (f32[192,4,8,128]{3,2,1,0:T(8,128)S(1)}, f32[192,4,8,128]{3,2,1,0:T(8,128)}, u32[]{:S(2)}) copy-start(f32[192,4,8,128]{3,2,1,0:T(8,128)} %param.5) | copy-start | bytes 9437188
  2.5 1.0 %copy-start.1 = (f32[32,4,8,128]{3,2,1,0:T(8,128)S(1)}, f32[32,4,8,128]{3,2,1,0:T(8,128)}, u32[]{:S(2)}) copy-start(f32[32,4,8,128]{3,2,1,0:T(8,128)} %noise.1) | copy-start | bytes 1572868
  3.6 0.7 %copy-start.2 = (f32[4,8,128]{2,1,0:T(8,128)S(1)}, f32[4,8,128]{2,1,0:T(8,128)}, u32[]{:S(2)}) copy-start(f32[4,8,128]{2,1,0:T(8,128)} %cond.1) | copy-start | bytes 49156
  4.3 0.7 %copy-start.3 = (f32[4,8,128]{2,1,0:T(8,128)S(1)}, f32[4,8,128]{2,1,0:T(8,128)}, u32[]{:S(2)}) copy-start(f32[4,8,128]{2,1,0:T(8,128)} %react.1) | copy-start | bytes 49156

commit v2 on v1

--- a/solution.py
+++ b/solution.py
@@ -9,6 +9,7 @@
 
 MESH = pl.DeviceIdType.MESH
 GROUP = 8
+VMEM_GRANT = 63 * 1024 * 1024
 F32 = jnp.float32
 BF16 = jnp.bfloat16
 
@@ -262,7 +263,7 @@
     (field, field2, image, stored, react_v, coef, high, low, flat_image, residual, chol,
      x_in1, x_in2, y_out1, y_in1, y_out2, y_in2, z_out1, z_in1, z_out2, z_in2,
      c_data, c_landed, c_crossed, c_result, g_data, g_landed, g_crossed, g_result,
-     in_sems, h_send1, h_recv1, h_send2, h_recv2, *sum_sems) = scratch
+     in_sems, out_sems, h_send1, h_recv1, h_send2, h_recv2, *sum_sems) = scratch
     columns, span = field2.shape[0], field2.shape[1]
     plane = span * 8
     kept = basis.shape[0] // plane
@@ -315,23 +316,6 @@
         high[0:kept, at * 128 : (at + 1) * 128] = one
         low[0:kept, at * 128 : (at + 1) * 128] = two
 
-    chunk = 1024
-    g_one = jnp.zeros((kept, 256), F32)
-    g_two = jnp.zeros((kept, 256), F32)
-    for at in range(0, cells, chunk):
-        right = high[:, at : at + chunk]
-        g_one = g_one + dot(high[0:kept, at : at + chunk], right, NT)
-        g_two = g_two + dot(low[0:kept, at : at + chunk], right, NT)
-    turned = jnp.transpose(jnp.concatenate([g_two, jnp.zeros((256 - kept, 256), F32)], axis=0))
-    g_local = g_one + g_two + turned[0:kept]
-    for at in range(kept // 8):
-        for half in range(2):
-            g_data[2 * at + half] = g_local[8 * at : 8 * at + 8, 128 * half : 128 * half + 128]
-
-    c_sum = Sum(owners, others, c_data, c_landed, c_crossed, c_result, sum_sems[0:6])
-    g_sum = Sum(owners, others, g_data, g_landed, g_crossed, g_result, sum_sems[6:12])
-    g_sum.scatter()
-
     load_react.wait()
     rim1.arrive()
     theta = field[columns]
@@ -382,7 +366,24 @@
     lo, hi = pack_z(field2[...].reshape(tiles, 8, 128), tiles)
     z_out2[0, 0], z_out2[1, 0] = lo, hi
     rim2.start(2)
-    g_sum.cross()
+
+    chunk = 1024
+    g_one = jnp.zeros((kept, 256), F32)
+    g_two = jnp.zeros((kept, 256), F32)
+    for at in range(0, cells, chunk):
+        right = high[:, at : at + chunk]
+        g_one = g_one + dot(high[0:kept, at : at + chunk], right, NT)
+        g_two = g_two + dot(low[0:kept, at : at + chunk], right, NT)
+    turned = jnp.transpose(jnp.concatenate([g_two, jnp.zeros((256 - kept, 256), F32)], axis=0))
+    g_local = g_one + g_two + turned[0:kept]
+    for at in range(kept // 8):
+        for half in range(2):
+            g_data[2 * at + half] = g_local[8 * at : 8 * at + 8, 128 * half : 128 * half + 128]
+
+    c_sum = Sum(owners, others, c_data, c_landed, c_crossed, c_result, sum_sems[0:6])
+    g_sum = Sum(owners, others, g_data, g_landed, g_crossed, g_result, sum_sems[6:12])
+    g_sum.scatter()
+
     rim2.arrive()
 
     def second_step(group, carry):
@@ -408,12 +409,12 @@
     for at in range(columns // 8):
         for half in range(2):
             c_data[2 * at + half] = c_local[8 * at : 8 * at + 8, 128 * half : 128 * half + 128]
+    g_sum.cross()
     c_sum.scatter()
     g_sum.gather()
     c_sum.cross()
+    g_sum.finish()
     c_sum.gather()
-    g_sum.finish()
-    c_sum.finish()
 
     def whole(total, rows):
         tiles_of = total[...].reshape(rows // 4, 8, 128)
@@ -425,17 +426,27 @@
             axis=0,
         )
 
-    g_full = jnp.concatenate(
-        [whole(g_result, kept) * scale, jnp.zeros((256 - kept, 256), F32)], axis=0
+    eye = jnp.where(
+        lanes_of((kept, 256)) == lax.broadcasted_iota(jnp.int32, (kept, 256), 0), 1.0, 0.0
+    ).astype(F32)
+    h_one = jnp.concatenate(
+        [eye - whole(g_result, kept) * scale, jnp.zeros((256 - kept, 256), F32)], axis=0
     )
+    h_two = dot_full(h_one, h_one, NN)
+    h_sum = h_one + h_two + dot_full(h_one, h_two, NN)
+    h_high, h_low = split(jnp.concatenate([h_one, h_sum], axis=1))
+
+    c_sum.finish()
     c_full = whole(c_result, columns) * scale
     lane = lanes_of((columns, 256))
     c_one = jnp.where(lane < kept, c_full, 0.0)
     square = c_full[:, kept : kept + columns]
-    total = 2.0 * c_one - dot_full(c_one, g_full, NN)
-    rest = c_one - dot_full(total, g_full, NN)
-    gram = square - dot_full(c_one, total, NT) - dot_full(total, rest, NT)
-    proj[...] = jnp.transpose(total)[0:kept, :]
+    c_both = jnp.concatenate(split(c_one), axis=0)
+    moved = dot(c_both, h_high, NN) + dot(c_both, h_low, NN)
+    moved = moved[0:columns] + moved[columns:]
+    total = c_one + moved[:, 0:256]
+    gram = square - dot_full(c_one + moved[:, 256:], c_one, NT)
+    proj[...] = total[:, 0:kept]
 
     p_high, p_low = split(total)
     p_both = jnp.concatenate([p_high, p_low], axis=0)[:, 0:kept]
@@ -449,25 +460,61 @@
     row = lax.broadcasted_iota(jnp.int32, wide, 0)
     table = jnp.where(lane == row + columns, 1.0, 0.0).astype(F32)
     table = table + jnp.concatenate([gram, jnp.zeros((columns, 128 - columns), F32)], axis=1)
-    for k in range(columns):
-        column = jnp.broadcast_to(table[:, k : k + 1], wide)
-        root = lax.rsqrt(column[k : k + 1, :])
-        line = table[k : k + 1, :] * root
-        chol[k : k + 1, :] = line
-        table = table - (column * root) * line
+    step = 8
+    for first in range(0, columns, step):
+        ahead = [
+            jnp.broadcast_to(table[:, first + j : first + j + 1], wide) for j in range(step)
+        ]
+        for j in range(step):
+            k = first + j
+            root = lax.rsqrt(ahead[j][k : k + 1, :])
+            column = ahead[j] * root
+            line = table[k : k + 1, :] * root
+            chol[k : k + 1, :] = line
+            table = table - column * line
+            for m in range(j + 1, step):
+                ahead[m] = ahead[m] - column * column[first + m : first + m + 1, :]
     done = chol[...]
     factor[...] = jnp.where(lane >= row, done, 0.0)[:, 0:columns]
-    inverse = done[:, columns : 2 * columns]
-    for at in range(0, cells, chunk):
-        here = slice(at, at + chunk)
-        part = dot_full(inverse, residual[:, here], NN)
-        for k in range(chunk // 128):
-            out[pl.ds(at // 128 + k, columns, stride=plane), :] = part[:, 128 * k : 128 * k + 128]
+    inverse = jnp.concatenate(split(done[:, columns : 2 * columns]), axis=0)
+    copies = []
+    for x in range(span):
+        here = slice(x * 1024, x * 1024 + 1024)
+        one, two = split(residual[:, here])
+        part = dot(inverse, one, NN) + dot(inverse, two, NN)
+        part = part[0:columns] + part[columns:]
+        for k in range(8):
+            image_rows[pl.ds(x * 8 + k, columns, stride=plane), :] = part[:, 128 * k : 128 * k + 128]
+        copies.append(pltpu.make_async_copy(image.at[:, x], out.at[:, x], out_sems.at[x]))
+        copies[-1].start()
+    for copy in copies:
+        copy.wait()
 
     rim1.drain()
     rim2.drain()
     g_sum.drain()
     c_sum.drain()
+
+
+def hand_over_kernel(*refs):
+    sems = refs[6]
+    copies = [pltpu.make_async_copy(refs[i], refs[3 + i], sems.at[i]) for i in range(3)]
+    for copy in copies:
+        copy.start()
+    for copy in copies:
+        copy.wait()
+
+
+def hand_over(*arrays):
+    return pl.pallas_call(
+        hand_over_kernel,
+        out_shape=tuple(jax.ShapeDtypeStruct(a.shape, a.dtype) for a in arrays),
+        in_specs=[pl.BlockSpec(memory_space=pl.ANY)] * 3,
+        out_specs=tuple([pl.BlockSpec(memory_space=pl.ANY)] * 3),
+        scratch_shapes=[pltpu.SemaphoreType.DMA((3,))],
+        compiler_params=pltpu.CompilerParams(vmem_limit_bytes=VMEM_GRANT),
+        name="hand_over",
+    )(*arrays)
 
 
 def shards(sizes, noise, basis, cond, react):
@@ -524,6 +571,7 @@
         *sum_buffers(c_tiles),
         *sum_buffers(g_tiles),
         dma(4),
+        dma(span),
         dma(6),
         dma(6),
         dma(6),
@@ -534,19 +582,24 @@
     out, factor, proj = pl.pallas_call(
         functools.partial(kernel, sizes, owners, others, cell_total),
         out_shape=(
-            jax.ShapeDtypeStruct((columns * plane, lanes), F32),
+            jax.ShapeDtypeStruct(noise.shape, F32),
             jax.ShapeDtypeStruct((columns, columns), F32),
-            jax.ShapeDtypeStruct((kept, columns), F32),
+            jax.ShapeDtypeStruct((columns, kept), F32),
         ),
         in_specs=[pl.BlockSpec(memory_space=pl.ANY)] * 4,
-        out_specs=tuple([pl.BlockSpec(memory_space=pltpu.VMEM)] * 3),
+        out_specs=(
+            pl.BlockSpec(memory_space=pl.ANY),
+            pl.BlockSpec(memory_space=pltpu.VMEM),
+            pl.BlockSpec(memory_space=pltpu.VMEM),
+        ),
         scratch_shapes=scratch,
         compiler_params=pltpu.CompilerParams(
-            collective_id=0, has_side_effects=True, vmem_limit_bytes=48 * 1024 * 1024
+            collective_id=0, has_side_effects=True, vmem_limit_bytes=VMEM_GRANT
         ),
         name="lanczos_step",
     )(noise, basis.reshape(kept * plane, lanes), cond, react)
-    return out.reshape(noise.shape), factor, proj
+    out, factor, proj = hand_over(out, factor, proj)
+    return out, factor, proj.T
 
 
 def solution(mesh):

time: 40.5 us -> 52.7 us (1.30)
  Pallas kernels: 33.1 us -> 51.9 us
  local copies, waits for them, and re-layouts: 6.45 us -> 0 us
    pallas_call x0 -> x1, Pallas kernels: none -> 18.5 us  [hand_over(): pl.pallas_call(hand_over_kernel, out_shape=tuple((jax.ShapeDtypeStruct(a....]
    unnamed x11 -> x0, local copies, waits for them, and re-layouts: 6.45 us -> none
where the time goes in v2:
time: 52.7 us; the launch traced here: 52.6 us
  Pallas kernels  51.9 us (98%)
  between operations  0.64 us (1%)
    pallas_call x1, Pallas kernels, shards(): pl.pallas_call(functools.partial(kernel, sizes, owners, others, cell_tota...  33.4 us
    pallas_call x1, Pallas kernels, hand_over(): pl.pallas_call(hand_over_kernel, out_shape=tuple((jax.ShapeDtypeStruct(a....  18.5 us

profile of v2, /device:TPU:0, one launch (start us, length us, event | category | flops | bytes accessed | tf_op | source)
XLA Modules:
  0.0 52.6 jit_solution(17526764628465020624)
XLA Ops:
  0.6 33.4 %lanczos_step.1 = (f32[32,4,8,128]{3,2,1,0:T(8,128)}, f32[32,32]{1,0:T(8,128)}, f32[32,192]{1,0:T(8,128)}) custom-call(f32[32,4,8,128]{3,2,1,0:T(8,128)} %noise.1, f32[6144,128]{1,0:T(8,128)} %bitcast.2, f32[4,8,128]{2,1,0:T(8,128)} %cond.1, f32[4,8,128]{2,1,0:T(8,128)} %react.1), custom_call_target="tpu_custom_call" | custom-call | tf_op jit(solution)/shard_map/lanczos_step/pallas_call | solution.py:582
  34.1 18.5 %hand_over.1 = (f32[32,4,8,128]{3,2,1,0:T(8,128)}, f32[32,32]{1,0:T(8,128)}, f32[32,192]{1,0:T(8,128)}) custom-call(f32[32,4,8,128]{3,2,1,0:T(8,128)} %get-tuple-element.9.refs_0_, f32[32,32]{1,0:T(8,128)} %get-tuple-element.10.refs_1_, f32[32,192]{1,0:T(8,128)} %get-tuple-element.11.refs_2_), custom_call_target="tpu_custom_call" | custom-call | tf_op jit(solution)/shard_map/hand_over/pallas_call | solution.py:509

commit v3 on v2

--- a/solution.py
+++ b/solution.py
@@ -259,8 +259,8 @@
 NN = ((1,), (0,))
 
 
-def kernel(sizes, owners, others, cell_total, noise, basis, cond, react, out, factor, proj, *scratch):
-    (field, field2, image, stored, react_v, coef, high, low, flat_image, residual, chol,
+def kernel(sizes, owners, others, cell_total, noise, basis, cond, react, left_over, chol, proj, *scratch):
+    (field, field2, image, stored, react_v, coef, high, low, flat_image, residual,
      x_in1, x_in2, y_out1, y_in1, y_out2, y_in2, z_out1, z_in1, z_out2, z_in2,
      c_data, c_landed, c_crossed, c_result, g_data, g_landed, g_crossed, g_result,
      in_sems, out_sems, h_send1, h_recv1, h_send2, h_recv2, *sum_sems) = scratch
@@ -338,7 +338,7 @@
     def apply(source, x_in, y_in, z_in, group):
         start = group * GROUP
         value = source[pl.ds(start, GROUP)]
-        shift = lax.rem(128 - group * (GROUP * span), 128)
+        shift = (128 - group * (GROUP * span)) % 128
         first = start * span
         around = neighbours(
             value,
@@ -346,20 +346,20 @@
             x_in[1, pl.ds(start, GROUP)],
             [y_in[0, pl.ds(first + i, 1), :] for i in range(GROUP * span)],
             [y_in[1, pl.ds(first + i, 1), :] for i in range(GROUP * span)],
-            pltpu.roll(z_in[0, 0], shift, 1),
-            pltpu.roll(z_in[1, 0], shift, 1),
+            pltpu.roll(z_in[0, 0], shift, 1) if shift else z_in[0, 0],
+            pltpu.roll(z_in[1, 0], shift, 1) if shift else z_in[1, 0],
         )
         result = react_v[...][None] * value
         for face, other in enumerate(around):
             result = result + coef[face][None] * (value - other)
         return start, result
 
-    def first_step(group, carry):
+    def first_step(group):
         start, result = apply(field, x_in1, y_in1, z_in1, group)
         field2[pl.ds(start, GROUP)] = result / coef[6][None]
-        return carry
-
-    lax.fori_loop(0, columns // GROUP, first_step, 0)
+
+    for group in range(columns // GROUP):
+        first_step(group)
     rim2.start(0)
     pack_y(field2.reshape(columns * plane, 128), tiles, y_out2)
     rim2.start(1)
@@ -386,12 +386,12 @@
 
     rim2.arrive()
 
-    def second_step(group, carry):
+    def second_step(group):
         start, result = apply(field2, x_in2, y_in2, z_in2, group)
         image[pl.ds(start, GROUP)] = result
-        return carry
-
-    lax.fori_loop(0, columns // GROUP, second_step, 0)
+
+    for group in range(columns // GROUP):
+        second_step(group)
     image_rows = image.reshape(columns * plane, 128)
     for at in range(plane):
         value = image_rows[pl.ds(at, columns, stride=plane), :]
@@ -454,6 +454,8 @@
         here = slice(at, at + chunk)
         part = dot(p_both, high[0:kept, here], NN) + dot(p_both, low[0:kept, here], NN)
         residual[:, here] = flat_image[:, here] - part[0:columns] - part[columns:]
+    write = pltpu.make_async_copy(residual, left_over, out_sems.at[0])
+    write.start()
 
     wide = (columns, 128)
     lane = lanes_of(wide)
@@ -474,47 +476,77 @@
             table = table - column * line
             for m in range(j + 1, step):
                 ahead[m] = ahead[m] - column * column[first + m : first + m + 1, :]
-    done = chol[...]
-    factor[...] = jnp.where(lane >= row, done, 0.0)[:, 0:columns]
-    inverse = jnp.concatenate(split(done[:, columns : 2 * columns]), axis=0)
-    copies = []
-    for x in range(span):
-        here = slice(x * 1024, x * 1024 + 1024)
-        one, two = split(residual[:, here])
-        part = dot(inverse, one, NN) + dot(inverse, two, NN)
-        part = part[0:columns] + part[columns:]
-        for k in range(8):
-            image_rows[pl.ds(x * 8 + k, columns, stride=plane), :] = part[:, 128 * k : 128 * k + 128]
-        copies.append(pltpu.make_async_copy(image.at[:, x], out.at[:, x], out_sems.at[x]))
-        copies[-1].start()
-    for copy in copies:
-        copy.wait()
-
+    write.wait()
     rim1.drain()
     rim2.drain()
     g_sum.drain()
     c_sum.drain()
 
 
-def hand_over_kernel(*refs):
-    sems = refs[6]
-    copies = [pltpu.make_async_copy(refs[i], refs[3 + i], sems.at[i]) for i in range(3)]
-    for copy in copies:
-        copy.start()
-    for copy in copies:
-        copy.wait()
-
-
-def hand_over(*arrays):
+def finish_kernel(left_over, chol, proj, out, factor, proj_out, rest, table, kept, upper, new, sems):
+    columns, span = new.shape[0], new.shape[1]
+    width = rest.shape[1] // span
+    load_table = pltpu.make_async_copy(chol, table, sems.at[0])
+    load_proj = pltpu.make_async_copy(proj, kept, sems.at[1])
+    loads = [
+        pltpu.make_async_copy(
+            left_over.at[:, pl.ds(x * width, width)], rest.at[:, pl.ds(x * width, width)], sems.at[4 + x]
+        )
+        for x in range(span)
+    ]
+    load_table.start()
+    for load in loads:
+        load.start()
+    load_proj.start()
+    load_table.wait()
+    done = table[...]
+    row = lax.broadcasted_iota(jnp.int32, done.shape, 0)
+    upper[...] = jnp.where(lanes_of(done.shape) >= row, done, 0.0)[:, 0:columns]
+    store_factor = pltpu.make_async_copy(upper, factor, sems.at[2])
+    store_factor.start()
+    load_proj.wait()
+    store_proj = pltpu.make_async_copy(kept, proj_out, sems.at[3])
+    store_proj.start()
+    inverse = jnp.concatenate(split(done[:, columns : 2 * columns]), axis=0)
+    rows = new.reshape(columns * span * 8, 128)
+    stores = []
+    for x in range(span):
+        loads[x].wait()
+        one, two = split(rest[:, x * width : (x + 1) * width])
+        part = dot(inverse, one, NN) + dot(inverse, two, NN)
+        part = part[0:columns] + part[columns:]
+        for k in range(8):
+            rows[pl.ds(x * 8 + k, columns, stride=span * 8), :] = part[:, 128 * k : 128 * k + 128]
+        stores.append(pltpu.make_async_copy(new.at[:, x], out.at[:, x], sems.at[4 + span + x]))
+        stores[-1].start()
+    for store in stores:
+        store.wait()
+    store_factor.wait()
+    store_proj.wait()
+
+
+def finish(left_over, chol, proj, shape):
+    columns, span = shape[0], shape[1]
     return pl.pallas_call(
-        hand_over_kernel,
-        out_shape=tuple(jax.ShapeDtypeStruct(a.shape, a.dtype) for a in arrays),
+        finish_kernel,
+        out_shape=(
+            jax.ShapeDtypeStruct(shape, F32),
+            jax.ShapeDtypeStruct((columns, columns), F32),
+            jax.ShapeDtypeStruct(proj.shape, F32),
+        ),
         in_specs=[pl.BlockSpec(memory_space=pl.ANY)] * 3,
         out_specs=tuple([pl.BlockSpec(memory_space=pl.ANY)] * 3),
-        scratch_shapes=[pltpu.SemaphoreType.DMA((3,))],
+        scratch_shapes=[
+            pltpu.VMEM(left_over.shape, F32),
+            pltpu.VMEM(chol.shape, F32),
+            pltpu.VMEM(proj.shape, F32),
+            pltpu.VMEM((columns, columns), F32),
+            pltpu.VMEM(shape, F32),
+            pltpu.SemaphoreType.DMA((4 + 2 * span,)),
+        ],
         compiler_params=pltpu.CompilerParams(vmem_limit_bytes=VMEM_GRANT),
-        name="hand_over",
-    )(*arrays)
+        name="new_block",
+    )(left_over, chol, proj)
 
 
 def shards(sizes, noise, basis, cond, react):
@@ -557,7 +589,6 @@
         pltpu.VMEM((256, cells), BF16),
         vmem(columns, cells),
         vmem(columns, cells),
-        vmem(columns, 128),
         vmem(2, columns + 1, 8, 128),
         vmem(2, columns, 8, 128),
         vmem(2, y_rows, 128),
@@ -571,7 +602,7 @@
         *sum_buffers(c_tiles),
         *sum_buffers(g_tiles),
         dma(4),
-        dma(span),
+        dma(1),
         dma(6),
         dma(6),
         dma(6),
@@ -579,11 +610,11 @@
         *sum_sems,
         *sum_sems,
     ]
-    out, factor, proj = pl.pallas_call(
+    left_over, chol, proj = pl.pallas_call(
         functools.partial(kernel, sizes, owners, others, cell_total),
         out_shape=(
-            jax.ShapeDtypeStruct(noise.shape, F32),
-            jax.ShapeDtypeStruct((columns, columns), F32),
+            jax.ShapeDtypeStruct((columns, cells), F32),
+            jax.ShapeDtypeStruct((columns, 128), F32),
             jax.ShapeDtypeStruct((columns, kept), F32),
         ),
         in_specs=[pl.BlockSpec(memory_space=pl.ANY)] * 4,
@@ -598,7 +629,7 @@
         ),
         name="lanczos_step",
     )(noise, basis.reshape(kept * plane, lanes), cond, react)
-    out, factor, proj = hand_over(out, factor, proj)
+    out, factor, proj = finish(left_over, chol, proj, noise.shape)
     return out, factor, proj.T
 
 

time: 52.7 us -> 35.4 us (0.67)
  Pallas kernels: 51.9 us -> 34.5 us
    pallas_call x1, Pallas kernels: 18.5 us -> 2.88 us  [finish(): pl.pallas_call(finish_kernel, out_shape=(jax.ShapeDtypeStruct(shape, F32)...]
    pallas_call x1, Pallas kernels: 33.4 us -> 31.6 us  [shards(): pl.pallas_call(functools.partial(kernel, sizes, owners, others, cell_tota...]
where the time goes in v3:
time: 35.4 us; the launch traced here: 35.1 us
  Pallas kernels  34.5 us (97%)
  between operations  0.64 us (2%)
    pallas_call x1, Pallas kernels, shards(): pl.pallas_call(functools.partial(kernel, sizes, owners, others, cell_tota...  31.6 us
    pallas_call x1, Pallas kernels, finish(): pl.pallas_call(finish_kernel, out_shape=(jax.ShapeDtypeStruct(shape, F32)...  2.88 us

profile of v3, /device:TPU:0, one launch (start us, length us, event | category | flops | bytes accessed | tf_op | source)
XLA Modules:
  0.0 35.1 jit_solution(17572149423931802234)
XLA Ops:
  0.6 31.6 %lanczos_step.1 = (f32[32,4096]{1,0:T(8,128)}, f32[32,128]{1,0:T(8,128)}, f32[32,192]{1,0:T(8,128)}) custom-call(f32[32,4,8,128]{3,2,1,0:T(8,128)} %noise.1, f32[6144,128]{1,0:T(8,128)} %bitcast.2, f32[4,8,128]{2,1,0:T(8,128)} %cond.1, f32[4,8,128]{2,1,0:T(8,128)} %react.1), custom_call_target="tpu_custom_call" | custom-call | tf_op jit(solution)/shard_map/lanczos_step/pallas_call | solution.py:613
  32.2 2.9 %new_block.1 = (f32[32,4,8,128]{3,2,1,0:T(8,128)}, f32[32,32]{1,0:T(8,128)}, f32[32,192]{1,0:T(8,128)}) custom-call(f32[32,4096]{1,0:T(8,128)} %get-tuple-element.9.left_over, f32[32,128]{1,0:T(8,128)} %get-tuple-element.10.chol, f32[32,192]{1,0:T(8,128)} %get-tuple-element.11.proj), custom_call_target="tpu_custom_call" | custom-call | tf_op jit(solution)/shard_map/new_block/pallas_call | solution.py:530

commit v4 on v3

--- a/solution.py
+++ b/solution.py
@@ -269,6 +269,7 @@
     kept = basis.shape[0] // plane
     cells = plane * 128
     tiles = columns * span
+    corner = kept - 128
     scale = 1.0 / cell_total
 
     load_noise = pltpu.make_async_copy(noise, field.at[pl.ds(0, columns)], in_sems.at[0])
@@ -377,8 +378,9 @@
     turned = jnp.transpose(jnp.concatenate([g_two, jnp.zeros((256 - kept, 256), F32)], axis=0))
     g_local = g_one + g_two + turned[0:kept]
     for at in range(kept // 8):
-        for half in range(2):
-            g_data[2 * at + half] = g_local[8 * at : 8 * at + 8, 128 * half : 128 * half + 128]
+        g_data[at] = g_local[8 * at : 8 * at + 8, 0:128]
+    for at in range(corner // 8):
+        g_data[kept // 8 + at] = g_local[128 + 8 * at : 136 + 8 * at, 128:256]
 
     c_sum = Sum(owners, others, c_data, c_landed, c_crossed, c_result, sum_sems[0:6])
     g_sum = Sum(owners, others, g_data, g_landed, g_crossed, g_result, sum_sems[6:12])
@@ -392,6 +394,7 @@
 
     for group in range(columns // GROUP):
         second_step(group)
+    g_sum.cross()
     image_rows = image.reshape(columns * plane, 128)
     for at in range(plane):
         value = image_rows[pl.ds(at, columns, stride=plane), :]
@@ -409,7 +412,6 @@
     for at in range(columns // 8):
         for half in range(2):
             c_data[2 * at + half] = c_local[8 * at : 8 * at + 8, 128 * half : 128 * half + 128]
-    g_sum.cross()
     c_sum.scatter()
     g_sum.gather()
     c_sum.cross()
@@ -426,14 +428,25 @@
             axis=0,
         )
 
-    eye = jnp.where(
-        lanes_of((kept, 256)) == lax.broadcasted_iota(jnp.int32, (kept, 256), 0), 1.0, 0.0
-    ).astype(F32)
-    h_one = jnp.concatenate(
-        [eye - whole(g_result, kept) * scale, jnp.zeros((256 - kept, 256), F32)], axis=0
+    g_tiles = g_result[...].reshape(kept // 8 + corner // 8, 8, 128)
+    g_left = jnp.concatenate([g_tiles[at] for at in range(kept // 8)], axis=0)
+    g_corner = jnp.concatenate([g_tiles[kept // 8 + at] for at in range(corner // 8)], axis=0)
+    blank = jnp.zeros((128 - corner, 128), F32)
+    g_right = jnp.concatenate(
+        [jnp.transpose(jnp.concatenate([g_left[128:], blank], axis=0)), g_corner, blank], axis=0
     )
-    h_two = dot_full(h_one, h_one, NN)
-    h_sum = h_one + h_two + dot_full(h_one, h_two, NN)
+    g_full = jnp.concatenate([jnp.concatenate([g_left, blank], axis=0), g_right], axis=1)
+    square_row = lax.broadcasted_iota(jnp.int32, (256, 256), 0)
+    eye = jnp.where((lanes_of((256, 256)) == square_row) & (square_row < kept), 1.0, 0.0)
+    h_one = eye.astype(F32) - g_full * scale
+    one_high, one_low = split(h_one)
+
+    def times_h(left):
+        high_part, low_part = split(left)
+        return dot(high_part, one_high, NN) + dot(low_part, one_high, NN) + dot(high_part, one_low, NN)
+
+    h_two = times_h(h_one)
+    h_sum = h_one + h_two + times_h(h_two)
     h_high, h_low = split(jnp.concatenate([h_one, h_sum], axis=1))
 
     c_sum.finish()
@@ -441,28 +454,26 @@
     lane = lanes_of((columns, 256))
     c_one = jnp.where(lane < kept, c_full, 0.0)
     square = c_full[:, kept : kept + columns]
-    c_both = jnp.concatenate(split(c_one), axis=0)
+    c_high, c_low = split(c_one)
+    c_both = jnp.concatenate([c_high, c_low], axis=0)
     moved = dot(c_both, h_high, NN) + dot(c_both, h_low, NN)
     moved = moved[0:columns] + moved[columns:]
     total = c_one + moved[:, 0:256]
-    gram = square - dot_full(c_one + moved[:, 256:], c_one, NT)
+    taken = jnp.concatenate(split(c_one + moved[:, 256:]), axis=0)
+    taken = dot(taken, c_high, NT) + dot(taken, c_low, NT)
+    gram = square - taken[0:columns] - taken[columns:]
     proj[...] = total[:, 0:kept]
 
     p_high, p_low = split(total)
     p_both = jnp.concatenate([p_high, p_low], axis=0)[:, 0:kept]
-    for at in range(0, cells, chunk):
-        here = slice(at, at + chunk)
-        part = dot(p_both, high[0:kept, here], NN) + dot(p_both, low[0:kept, here], NN)
-        residual[:, here] = flat_image[:, here] - part[0:columns] - part[columns:]
-    write = pltpu.make_async_copy(residual, left_over, out_sems.at[0])
-    write.start()
-
     wide = (columns, 128)
     lane = lanes_of(wide)
     row = lax.broadcasted_iota(jnp.int32, wide, 0)
     table = jnp.where(lane == row + columns, 1.0, 0.0).astype(F32)
     table = table + jnp.concatenate([gram, jnp.zeros((columns, 128 - columns), F32)], axis=1)
     step = 8
+    width = cells * step // columns
+    writes = []
     for first in range(0, columns, step):
         ahead = [
             jnp.broadcast_to(table[:, first + j : first + j + 1], wide) for j in range(step)
@@ -476,7 +487,18 @@
             table = table - column * line
             for m in range(j + 1, step):
                 ahead[m] = ahead[m] - column * column[first + m : first + m + 1, :]
-    write.wait()
+        at = first // step * width
+        here = slice(at, at + width)
+        part = dot(p_both, high[0:kept, here], NN) + dot(p_both, low[0:kept, here], NN)
+        residual[:, here] = flat_image[:, here] - part[0:columns] - part[columns:]
+        writes.append(
+            pltpu.make_async_copy(
+                residual.at[:, here], left_over.at[:, here], out_sems.at[first // step]
+            )
+        )
+        writes[-1].start()
+    for write in writes:
+        write.wait()
     rim1.drain()
     rim2.drain()
     g_sum.drain()
@@ -555,7 +577,7 @@
     plane = span * rows
     cells = plane * lanes
     cell_total = float(cells * sizes["gx"] * sizes["gy"] * sizes["gz"])
-    c_tiles, g_tiles = columns // 4, kept // 4
+    c_tiles, g_tiles = columns // 4, kept // 8 + (kept - 128) // 8
     own, rest, count = [], [], 1
     for axis in ("gx", "gy", "gz"):
         if c_tiles % (count * sizes[axis]) == 0:
@@ -602,7 +624,7 @@
         *sum_buffers(c_tiles),
         *sum_buffers(g_tiles),
         dma(4),
-        dma(1),
+        dma(columns // 8),
         dma(6),
         dma(6),
         dma(6),

time: 35.4 us -> 35.2 us (level)
  no operation moved by 1% of the time
where the time goes in v4:
time: 35.2 us; the launch traced here: 34.9 us
  Pallas kernels  34.3 us (97%)
  between operations  0.64 us (2%)
    pallas_call x1, Pallas kernels, shards(): pl.pallas_call(functools.partial(kernel, sizes, owners, others, cell_tota...  31.4 us
    pallas_call x1, Pallas kernels, finish(): pl.pallas_call(finish_kernel, out_shape=(jax.ShapeDtypeStruct(shape, F32)...  2.88 us

profile of v4, /device:TPU:0, one launch (start us, length us, event | category | flops | bytes accessed | tf_op | source)
XLA Modules:
  0.0 34.9 jit_solution(14296970159080254414)
XLA Ops:
  0.6 31.4 %lanczos_step.1 = (f32[32,4096]{1,0:T(8,128)}, f32[32,128]{1,0:T(8,128)}, f32[32,192]{1,0:T(8,128)}) custom-call(f32[32,4,8,128]{3,2,1,0:T(8,128)} %noise.1, f32[6144,128]{1,0:T(8,128)} %bitcast.2, f32[4,8,128]{2,1,0:T(8,128)} %cond.1, f32[4,8,128]{2,1,0:T(8,128)} %react.1), custom_call_target="tpu_custom_call" | custom-call | tf_op jit(solution)/shard_map/lanczos_step/pallas_call | solution.py:635
  32.0 2.9 %new_block.1 = (f32[32,4,8,128]{3,2,1,0:T(8,128)}, f32[32,32]{1,0:T(8,128)}, f32[32,192]{1,0:T(8,128)}) custom-call(f32[32,4096]{1,0:T(8,128)} %get-tuple-element.9.left_over, f32[32,128]{1,0:T(8,128)} %get-tuple-element.10.chol, f32[32,192]{1,0:T(8,128)} %get-tuple-element.11.proj), custom_call_target="tpu_custom_call" | custom-call | tf_op jit(solution)/shard_map/new_block/pallas_call | solution.py:552

commit v5 on v4

--- a/solution.py
+++ b/solution.py
@@ -369,12 +369,12 @@
     rim2.start(2)
 
     chunk = 1024
-    g_one = jnp.zeros((kept, 256), F32)
-    g_two = jnp.zeros((kept, 256), F32)
+    g_both = jnp.zeros((2 * kept, 256), F32)
     for at in range(0, cells, chunk):
-        right = high[:, at : at + chunk]
-        g_one = g_one + dot(high[0:kept, at : at + chunk], right, NT)
-        g_two = g_two + dot(low[0:kept, at : at + chunk], right, NT)
+        here = slice(at, at + chunk)
+        left = jnp.concatenate([high[0:kept, here], low[0:kept, here]], axis=0)
+        g_both = g_both + dot(left, high[:, here], NT)
+    g_one, g_two = g_both[0:kept], g_both[kept:]
     turned = jnp.transpose(jnp.concatenate([g_two, jnp.zeros((256 - kept, 256), F32)], axis=0))
     g_local = g_one + g_two + turned[0:kept]
     for at in range(kept // 8):
@@ -403,12 +403,15 @@
         high[kept : kept + columns, at * 128 : (at + 1) * 128] = one
         low[kept : kept + columns, at * 128 : (at + 1) * 128] = two
 
-    both = jnp.zeros((2 * columns, 256), F32)
+    both = jnp.zeros((512, 128), F32)
+    unused = jnp.zeros((128 - 2 * columns, chunk), BF16)
     for at in range(0, cells, chunk):
         here = slice(at, at + chunk)
-        left = jnp.concatenate([high[kept : kept + columns, here], low[kept : kept + columns, here]], axis=0)
-        both = both + dot(left, high[:, here], NT) + dot(left, low[:, here], NT)
-    c_local = both[0:columns] + both[columns:]
+        right = [high[kept : kept + columns, here], low[kept : kept + columns, here], unused]
+        left = jnp.concatenate([high[:, here], low[:, here]], axis=0)
+        both = both + dot(left, jnp.concatenate(right, axis=0), NT)
+    both = jnp.transpose(both[0:256] + both[256:])
+    c_local = both[0:columns] + both[columns : 2 * columns]
     for at in range(columns // 8):
         for half in range(2):
             c_data[2 * at + half] = c_local[8 * at : 8 * at + 8, 128 * half : 128 * half + 128]

time: 35.2 us -> 35 us (level)
  no operation moved by 1% of the time
where the time goes in v5:
time: 35 us; the launch traced here: 34.8 us
  Pallas kernels  34.2 us (98%)
  between operations  0.64 us (2%)
    pallas_call x1, Pallas kernels, shards(): pl.pallas_call(functools.partial(kernel, sizes, owners, others, cell_tota...  31.3 us
    pallas_call x1, Pallas kernels, finish(): pl.pallas_call(finish_kernel, out_shape=(jax.ShapeDtypeStruct(shape, F32)...  2.88 us

profile of v5, /device:TPU:0, one launch (start us, length us, event | category | flops | bytes accessed | tf_op | source)
XLA Modules:
  0.0 34.8 jit_solution(4524245498855849296)
XLA Ops:
  0.6 31.3 %lanczos_step.1 = (f32[32,4096]{1,0:T(8,128)}, f32[32,128]{1,0:T(8,128)}, f32[32,192]{1,0:T(8,128)}) custom-call(f32[32,4,8,128]{3,2,1,0:T(8,128)} %noise.1, f32[6144,128]{1,0:T(8,128)} %bitcast.2, f32[4,8,128]{2,1,0:T(8,128)} %cond.1, f32[4,8,128]{2,1,0:T(8,128)} %react.1), custom_call_target="tpu_custom_call" | custom-call | tf_op jit(solution)/shard_map/lanczos_step/pallas_call | solution.py:638
  31.9 2.9 %new_block.1 = (f32[32,4,8,128]{3,2,1,0:T(8,128)}, f32[32,32]{1,0:T(8,128)}, f32[32,192]{1,0:T(8,128)}) custom-call(f32[32,4096]{1,0:T(8,128)} %get-tuple-element.9.left_over, f32[32,128]{1,0:T(8,128)} %get-tuple-element.10.chol, f32[32,192]{1,0:T(8,128)} %get-tuple-element.11.proj), custom_call_target="tpu_custom_call" | custom-call | tf_op jit(solution)/shard_map/new_block/pallas_call | solution.py:555
